TPU v7x, 256 devices: a whole 4x4x8 slice. The times are simulated.
256 devices in a mesh: cfg: 2 (over x_lo), seq: 128 (over y, z, x_hi, core).
Axes of the slice: x: 4 (x_hi: 2, x_lo: 2; x = x_hi * 2 + x_lo), y: 4, z: 8, core: 2. Of those that a mesh axis runs over, the one named last changes fastest.
Arguments:
- coarse_hidden: bfloat16 [2, 256, 64, 2048], P('cfg', 'seq'), may hold values from -6 to 6
- coarse_modulation: float32 [2, 2, 2048], P('cfg'), may hold values from -3 to 3
- final_weight: bfloat16 [2048, 32], replicated, may hold values from -0.125 to 0.125
- coarse_latent: float32 [256, 2048], P('seq'), may hold values from -6 to 6
- step_index: int32 [1], replicated, may hold values from 0 to 49
- guide_index: int32 [1], replicated, may hold values from 0 to 4095
- guide_scales: float32 [4096], replicated, may hold values from 1.5 to 6
- upsample_weight: float32 [288, 32], replicated, may hold values from -0.375 to 0.375
- upsample_bias: float32 [32], replicated, may hold values from -3 to 3
- embed_weight: bfloat16 [32, 2048], replicated, may hold values from -1 to 1
- embed_bias: float32 [2048], replicated, may hold values from -3 to 3
- fine_modulation: float32 [3, 2048], replicated, may hold values from -3 to 3
- project_weight: bfloat16 [2048, 3072], P(('cfg', 'seq')), may hold values from -0.125 to 0.125
- query_gain: float32 [128], replicated, may hold values from 0.25 to 1.75
- key_gain: float32 [128], replicated, may hold values from 0.25 to 1.75
- text_keys: bfloat16 [256, 1024], replicated, may hold values from -6 to 6
- text_values: bfloat16 [256, 1024], replicated, may hold values from -6 to 6
- text_length: int32 [1], replicated, may hold values from 192 to 256
- output_weight: bfloat16 [1024, 2048], P(None, ('cfg', 'seq')), may hold values from -0.1875 to 0.1875
Outputs:
- guided_velocity: float32 [256, 2048], P('seq')
- fine_latent: float32 [256, 2, 4096], P('seq', 'cfg')
- fine_hidden: bfloat16 [256, 2, 128, 2048], P('seq', 'cfg')
All inputs are finite; a program needn't handle non-finite values.
Results may differ from a plain program's by a relative error of at most 0.0053.
Values may be sent and summed in bfloat16 or wider, within the bound.
A program may use at most 128 MiB of HBM per device.

v0:
```python
import jax
import jax.numpy as jnp
from jax import lax
from jax.sharding import PartitionSpec as P

HEADS = 8
STEPS = 50
epsilon = 1e-06
flow_shift = 5.0
highest = lax.Precision.HIGHEST


def from_partner(shard, axis, bit):
    return lax.ppermute(shard, axis, [(i, i ^ 1 << bit) for i in range(lax.axis_size(axis))])


def with_halo(block, sides, width):
    for axis, dim in sides:
        count = lax.axis_size(axis)
        forward = [(i, i + 1) for i in range(count - 1)]
        backward = [(target, source) for source, target in forward]
        low = lax.ppermute(
            lax.slice_in_dim(block, block.shape[dim] - width, None, axis=dim), axis, forward
        )
        high = lax.ppermute(lax.slice_in_dim(block, 0, width, axis=dim), axis, backward)
        block = jnp.concatenate([low, block, high], axis=dim)
    return block


def layer_norm(values):
    centred = values - jnp.mean(values, -1, keepdims=True)
    return centred * lax.rsqrt(jnp.mean(centred * centred, -1, keepdims=True) + epsilon)


def rms_heads(values, gain_vector, head_width):
    shaped = values.reshape(values.shape[0], -1, head_width)
    scaled = (
        shaped * lax.rsqrt(jnp.mean(shaped * shaped, -1, keepdims=True) + epsilon) * gain_vector
    )
    return scaled.reshape(values.shape[0], -1)


def sigma_at(step_value):
    fraction = 1.0 - step_value.astype(jnp.float32) / STEPS
    return flow_shift * fraction / (1.0 + (flow_shift - 1.0) * fraction)


def pick_scale(scale_table, slot_index):
    slots = jnp.arange(scale_table.shape[0], dtype=jnp.int32)
    return jnp.sum(jnp.where(slots == slot_index, scale_table, 0.0))


def attend(queries, image_keys, image_values, text_keys, text_values, image_mask, text_mask, heads):
    head_width = queries.shape[1] // heads
    score_scale = head_width ** (-0.5)
    dims = (((1,), (1,)), ((), ()))

    def one_head(head_index):
        column_start = head_index * head_width
        query_part = lax.dynamic_slice_in_dim(queries, column_start, head_width, 1)
        key_part = lax.dynamic_slice_in_dim(image_keys, column_start, head_width, 1)
        value_part = lax.dynamic_slice_in_dim(image_values, column_start, head_width, 1)
        text_key_part = lax.dynamic_slice_in_dim(text_keys, column_start, head_width, 1)
        text_value_part = lax.dynamic_slice_in_dim(text_values, column_start, head_width, 1)
        image_scores = (
            lax.dot_general(query_part, key_part, dims, preferred_element_type=jnp.float32)
            * score_scale
        )
        text_scores = (
            lax.dot_general(query_part, text_key_part, dims, preferred_element_type=jnp.float32)
            * score_scale
        )
        image_weights = jnp.where(image_mask, jnp.exp(image_scores), 0.0)
        text_weights = jnp.where(text_mask, jnp.exp(text_scores), 0.0)
        denominator = jnp.sum(image_weights, 1, keepdims=True) + jnp.sum(
            text_weights, 1, keepdims=True
        )
        image_weights = (image_weights / denominator).astype(jnp.bfloat16)
        text_weights = (text_weights / denominator).astype(jnp.bfloat16)
        return jnp.dot(image_weights, value_part, preferred_element_type=jnp.float32) + jnp.dot(
            text_weights, text_value_part, preferred_element_type=jnp.float32
        )

    stacked = lax.map(one_head, jnp.arange(heads, dtype=jnp.int32))
    return stacked.transpose(1, 0, 2).reshape(queries.shape[0], -1).astype(jnp.bfloat16)


def conv_rows(above, centre, below, upsample_weight, upsample_bias):
    tap_list = []
    for row_set in (above, centre, below):
        breadth = row_set.shape[1]
        padded = jnp.pad(row_set, ((0, 0), (1, 1), (0, 0)))
        for col_shift in range(3):
            tap_list.append(padded[:, col_shift : col_shift + breadth])
    patches = jnp.concatenate(tap_list, -1)
    flat_patches = patches.reshape(-1, patches.shape[-1])
    product = jnp.dot(flat_patches, upsample_weight, precision=highest).reshape(centre.shape)
    return product + upsample_bias + centre


def per_device(
    coarse_hidden,
    coarse_modulation,
    final_weight,
    coarse_latent,
    step_index,
    guide_index,
    guide_scales,
    upsample_weight,
    upsample_bias,
    embed_weight,
    embed_bias,
    fine_modulation,
    project_weight,
    query_gain,
    key_gain,
    text_keys,
    text_values,
    text_length,
    output_weight,
):
    row_count = coarse_hidden.shape[1]
    row_cells = coarse_hidden.shape[2]
    model_width = coarse_hidden.shape[3]
    channels = final_weight.shape[1]
    head_width = query_gain.shape[0]
    inner = project_weight.shape[1] // 3
    reach = max(row_count // 2, 1)
    branch = lax.axis_index("cfg")
    seq_index = lax.axis_index("seq")
    normed = layer_norm(coarse_hidden[0].astype(jnp.float32))
    modulated = (normed * (1.0 + coarse_modulation[0, 1]) + coarse_modulation[0, 0]).astype(
        jnp.bfloat16
    )
    velocity = jnp.dot(
        modulated.reshape(row_count * row_cells, model_width),
        final_weight,
        preferred_element_type=jnp.float32,
    ).reshape(row_count, row_cells * channels)
    partner = from_partner(velocity, "cfg", 0)
    conditional = jnp.where(branch == 0, velocity, partner)
    unconditional = jnp.where(branch == 0, partner, velocity)
    guidance = pick_scale(guide_scales, guide_index[0])
    guided = unconditional + guidance * (conditional - unconditional)
    stepped = coarse_latent + (sigma_at(step_index[0] + 1) - sigma_at(step_index[0])) * guided
    scale = 1.0 + fine_modulation[1]
    embed32 = embed_weight.astype(jnp.float32)
    embed_centred = embed32 - jnp.mean(embed32, -1, keepdims=True)
    bias_centred = embed_bias - jnp.mean(embed_bias)
    folded_left = jnp.concatenate(
        [embed_centred * scale, (bias_centred * scale)[None], fine_modulation[0][None]], 0
    )
    depth = project_weight.shape[0]
    device = branch * lax.axis_size("seq") + seq_index
    left_part = lax.dynamic_slice_in_dim(folded_left, device * depth, depth, 1)
    folded = lax.psum(
        jnp.dot(left_part, project_weight.astype(jnp.float32), precision=highest), ("cfg", "seq")
    )
    output_rows = lax.all_gather(output_weight.T, ("cfg", "seq"), axis=0, tiled=True)

    def embed_rows(grid_rows):
        grid_tokens = grid_rows.reshape(-1, channels).astype(jnp.bfloat16)
        centred = (
            jnp.dot(grid_tokens.astype(jnp.float32), embed_centred, precision=highest)
            + bias_centred
        )
        rstd = lax.rsqrt(jnp.mean(centred * centred, -1, keepdims=True) + epsilon)
        return (grid_tokens, rstd)

    def project(tokens_rstd, start, stop):
        tokens, rstd = tokens_rstd
        part = folded[:, start:stop]
        product = jnp.dot(tokens.astype(jnp.float32), part[:channels], precision=highest)
        return rstd * (product + part[channels]) + part[channels + 1]

    latent_grid = stepped.reshape(row_count, row_cells, channels)
    rim_width = reach + 1
    rimmed = with_halo(latent_grid, (("seq", 0),), rim_width)
    upsampled = jnp.repeat(jnp.repeat(rimmed, 2, 0), 2, 1)
    span = row_count + 2 * reach
    wide_grid = conv_rows(
        upsampled[1 : 1 + 2 * span],
        upsampled[2 : 2 + 2 * span],
        upsampled[3 : 3 + 2 * span],
        upsample_weight,
        upsample_bias,
    )
    grouped = wide_grid.reshape(span, 2, 2 * row_cells, channels)
    fine_grid = lax.dynamic_index_in_dim(
        grouped[reach : reach + row_count], branch, 1, keepdims=False
    )
    own = embed_rows(fine_grid)
    fine_state = jnp.dot(own[0], embed_weight, preferred_element_type=jnp.float32) + embed_bias
    around = embed_rows(wide_grid)
    token_count = own[0].shape[0]
    query_sum = project(own, 0, inner)
    key_sum = project(around, inner, 2 * inner)
    value_sum = project(around, 2 * inner, 3 * inner)
    queries = rms_heads(query_sum, query_gain, head_width).astype(jnp.bfloat16)
    keys = rms_heads(key_sum, key_gain, head_width).astype(jnp.bfloat16)
    values = value_sum.astype(jnp.bfloat16)
    image_keys, image_values = (keys, values)
    normed_text_keys = rms_heads(text_keys.astype(jnp.float32), key_gain, head_width).astype(
        jnp.bfloat16
    )
    key_count = image_keys.shape[0]
    query_rows = jnp.arange(token_count, dtype=jnp.int32) // (2 * row_cells)
    key_rows = jnp.arange(key_count, dtype=jnp.int32) // (4 * row_cells)
    distance = key_rows[None, :] - query_rows[:, None]
    global_rows = seq_index * row_count + key_rows - reach
    row_valid = (global_rows >= 0) & (global_rows < row_count * lax.axis_size("seq"))
    image_mask = (distance >= 0) & (distance <= 2 * reach) & row_valid[None, :]
    text_mask = (jnp.arange(text_keys.shape[0], dtype=jnp.int32) < text_length[0])[None, :]
    attended = attend(
        queries,
        image_keys,
        image_values,
        normed_text_keys,
        text_values,
        image_mask,
        text_mask,
        HEADS,
    )
    output_part = lax.dot_general(
        attended, output_rows, (((1,), (1,)), ((), ())), preferred_element_type=jnp.float32
    )
    fine_hidden = (fine_state + fine_modulation[2] * output_part).astype(jnp.bfloat16)
    fine_hidden = fine_hidden.reshape(row_count, 1, 2 * row_cells, model_width)
    fine_latent = fine_grid.reshape(row_count, 1, 2 * row_cells * channels)
    return (guided, fine_latent, fine_hidden)


def solution(mesh):
    placed = (
        P("cfg", "seq", None, None),
        P("cfg", None, None),
        P(),
        P("seq", None),
        P(),
        P(),
        P(),
        P(),
        P(),
        P(),
        P(),
        P(),
        P(("cfg", "seq"), None),
        P(),
        P(),
        P(),
        P(),
        P(),
        P(None, ("cfg", "seq")),
    )
    return jax.shard_map(
        per_device,
        mesh=mesh,
        in_specs=placed,
        out_specs=(P("seq", None), P("seq", "cfg", None), P("seq", "cfg", None, None)),
        check_vma=False,
    )
```

profile of v0, /device:TPU:32, one launch (start us, length us, event | category | flops | bytes accessed | tf_op | source)
XLA Modules:
  0.0 696.4 jit_solution(8204464123050728577)
XLA Ops:
  7.3 1.5 fusion.84
  10.8 1.3 reduce_sum.112
  13.5 2.0 fusion.65
  17.0 1.6 collective-permute-start
  23.5 1.3 multiply_add_fusion.1
  24.9 1.9 collective-permute-start.1
  27.4 6.0 collective-permute-start.2
  33.5 1.8 collective-permute-done.2
  39.3 1.2 fusion.28
  40.4 4.5 multiply_reduce_fusion
  45.0 223.4 %all-reduce.5.cloned.1.call-done = f32[34,3072]{1,0:T(8,128)} async-done(((f32[34,3072]{1,0:T(8,128)}), f32[34,3072]{1,0:T(8,128)}) %all-reduce.5.cloned.1.call-update) | async-done | bytes 417808 | tf_op jit(solution)/shard_map/psum | solution.py:156
  269.3 1.6 fusion.30
  271.7 3.4 bitcast_reduce_fusion
  275.9 1.1 fusion.23
  277.0 4.4 add_convert_fusion
  281.9 58.2 %while.11 = (s32[]{:T(128)}, bf16[8,256,128]{1,2,0:T(8,128)(2,1)}, s32[8]{0:T(128)}, bf16[256,1024]{1,0:T(8,128)(2,1)S(1)}, bf16[1024,1024]{0,1:T(8,128)(2,1)S(1...) while((s32[]{:T(128)}, bf16[8,256,128]{1,2,0:T(8,128)(2,1)}, ...), condition=%wide.region_14.15_spmd.clone, body=%wide.region_11.14_spmd.clone.sunk | while | flops 170786816 | bytes 4014055 | solution.py:84
  281.9 1.2 dynamic_slice.86
  284.7 1.3 fusion.102
  286.0 1.1 fusion.103
  287.1 1.3 fusion.104
  289.2 1.2 dynamic_slice.86
  291.9 1.3 fusion.102
  293.3 1.1 fusion.103
  294.3 1.3 fusion.104
  296.4 1.2 dynamic_slice.86
  299.2 1.3 fusion.102
  301.6 1.3 fusion.104
  303.7 1.2 dynamic_slice.86
  306.5 1.3 fusion.102
  308.9 1.3 fusion.104
  311.0 1.2 dynamic_slice.86
  313.8 1.3 fusion.102
  315.1 1.1 fusion.103
  316.2 1.3 fusion.104
  318.3 1.2 dynamic_slice.86
  321.0 1.3 fusion.102
  323.4 1.3 fusion.104
  325.5 1.2 dynamic_slice.86
  328.3 1.3 fusion.102
  329.6 1.1 fusion.103
  330.7 1.3 fusion.104
  332.8 1.2 dynamic_slice.86
  335.6 1.3 fusion.102
  336.9 1.1 fusion.103
  338.0 1.3 fusion.104
  340.1 344.3 %all-gather.2.cloned.1.call-done = bf16[2048,1024]{1,0:T(8,128)(2,1)} async-done(((bf16[8,1024]{1,0:T(8,128)(2,1)}), bf16[2048,1024]{1,0:T(8,128)(2,1)}) %all-gather.2.cloned.1.call-update) | async-done | bytes 4194320 | tf_op jit(solution)/shard_map/all_gather | solution.py:159
  684.4 3.6 convolution_multiply_fusion.2
  688.1 1.4 fusion.27
  (153 shorter events, 31.5 us)
Async XLA Ops:
  7.2 9.5 %copy-start = (bf16[2048,32]{0,1:T(8,128)(2,1)S(1)}, bf16[2048,32]{0,1:T(8,128)(2,1)}, u32[]{:S(2)}) copy-start(bf16[2048,32]{0,1:T(8,128)(2,1)} %param.23) | copy-start | bytes 393220
  7.2 8.4 %copy-start.1 = (bf16[1,2,64,2048]{3,2,1,0:T(8,128)(2,1)S(1)}, bf16[1,2,64,2048]{3,2,1,0:T(8,128)(2,1)}, u32[]{:S(2)}) copy-start(bf16[1,2,64,2048]{3,2,1,0:T(8,128)(2,1)} %param.21) | copy-start | bytes 1572868
  7.2 8.9 %copy-start.8 = (f32[1,2,2048]{2,1,0:T(2,128)S(1)}, f32[1,2,2048]{2,1,0:T(2,128)}, u32[]{:S(2)}) copy-start(f32[1,2,2048]{2,1,0:T(2,128)} %param.22) | copy-start | bytes 49156
  7.2 261.2 %all-reduce.5.cloned.1.call-start = ((), (), s32[]{:S(2)}) async-start(), calls=%async_computation | async-start | bytes 983040 | tf_op jit(solution)/shard_map/psum | solution.py:156
  13.4 6.4 copy-start.12
  13.5 6.5 copy-start.13
  13.5 6.5 copy-start.2
  15.5 668.9 %all-gather.2.cloned.1.call-start = ((), (), s32[]{:S(2)}) async-start(), calls=%async_computation.1 | async-start | bytes 4210688 | tf_op jit(solution)/shard_map/all_gather | solution.py:159
  17.0 6.4 collective-permute-start
  20.1 0.8 copy-start.9
  20.6 2.9 copy-start.10
  24.9 8.6 %collective-permute-start.1 = (f32[2,64,32]{2,1,0:T(8,128)S(1)}, f32[2,64,32]{2,1,0:T(8,128)S(1)}, u32[]{:S(2)}, u32[]{:S(2)}) collective-permute-start(f32[2,64,32]{2,1,0:T(8,128)S(1)} %reshape.230), channel_id=1, source_target_pairs={{0,1},{1,2},{2,3},{3,4},{4,5},{5,6},{6,7},{7,8},{8,9},{9,10},{10,1... | collective-permute-start | bytes 49160 | tf_op jit(solution)/shard_map/ppermute | solution.py:22
  27.4 7.9 %collective-permute-start.2 = (f32[2,64,32]{2,1,0:T(8,128)S(1)}, f32[2,64,32]{2,1,0:T(8,128)S(1)}, u32[]{:S(2)}, u32[]{:S(2)}) collective-permute-start(f32[2,64,32]{2,1,0:T(8,128)S(1)} %reshape.230), channel_id=1, source_target_pairs={{1,0},{2,1},{3,2},{4,3},{5,4},{6,5},{7,6},{8,7},{9,8},{10,9},{11,1... | collective-permute-start | bytes 49160 | tf_op jit(solution)/shard_map/ppermute | solution.py:25
  36.3 1.1 copy-start.7
  36.3 1.1 copy-start.11
  36.9 2.3 copy-start.3
  38.4 233.4 %copy-start.5 = (bf16[8,4,8,128]{3,2,1,0:T(8,128)(2,1)}, bf16[8,4,8,128]{3,2,1,0:T(8,128)(2,1)S(1)}, u32[]{:S(2)}) copy-start(bf16[8,4,8,128]{3,2,1,0:T(8,128)(2,1)S(1)} %convert_bitcast_fusion) | copy-start | bytes 196612
  275.9 1.1 copy-start.6
  684.4 3.6 copy-start.4
Sparse Core Ops, SparseCore 0:
  15.6 252.6 all-reduce.4
  270.3 414.1 all-gather.1
where the time goes:
time: 698 us; the launch traced here: 696 us
  waiting for transfers between devices  570 us (82%)
  matrix products  55 us (8%)
  local copies, waits for them, and re-layouts  21.8 us (3%)
  other arithmetic  18.2 us (3%)
  between operations  16.7 us (2%)
  starting transfers between devices  9.61 us (1%)
    all_gather x1, waiting for transfers between devices, per_device(): lax.all_gather(output_weight.T, ('cfg', 'seq'), axis=0, tiled=True)  344 us
    psum x1, waiting for transfers between devices, per_device(): lax.psum(jnp.dot(left_part, project_weight.astype(jnp.float32), precision...  223 us
  transfers between devices with their start and end apart: 5, of which 3 were waited for; matrix products, arithmetic and copies ran while one was open for 12% of the time, Pallas kernels for 0%

commit v1 on v0

--- a/solution.py
+++ b/solution.py
@@ -153,9 +153,9 @@
     depth = project_weight.shape[0]
     device = branch * lax.axis_size("seq") + seq_index
     left_part = lax.dynamic_slice_in_dim(folded_left, device * depth, depth, 1)
-    folded = lax.psum(
-        jnp.dot(left_part, project_weight.astype(jnp.float32), precision=highest), ("cfg", "seq")
-    )
+    folded = jnp.dot(left_part, project_weight.astype(jnp.float32), precision=highest)
+    for over in ("seq", "cfg"):
+        folded = lax.psum(folded, over)
     output_rows = lax.all_gather(output_weight.T, ("cfg", "seq"), axis=0, tiled=True)
 
     def embed_rows(grid_rows):

time: 698 us -> 1620 us (2.32)
  waiting for transfers between devices: 570 us -> 1490 us
    psum x1 -> x2, waiting for transfers between devices: 223 us -> 1180 us  [per_device(): folded = lax.psum(folded, over)]
    all_gather x1, waiting for transfers between devices: 344 us -> 309 us  [per_device(): lax.all_gather(output_weight.T, ('cfg', 'seq'), axis=0, tiled=True)]
  transfers between devices with their start and end apart: 5 -> 6, of which waited for: 3 -> 4; matrix products, arithmetic and copies ran while one was open for 12% -> 5% of each run, Pallas kernels for 0% -> 0%
where the time goes in v1:
time: 1620 us
  waiting for transfers between devices  1490 us (92%)
  matrix products  55 us (3%)
  local copies, waits for them, and re-layouts  21.8 us (1%)
  other arithmetic  18.2 us (1%)
  between operations  18.2 us (1%)
    psum x2, waiting for transfers between devices, per_device(): folded = lax.psum(folded, over)  1180 us
    all_gather x1, waiting for transfers between devices, per_device(): lax.all_gather(output_weight.T, ('cfg', 'seq'), axis=0, tiled=True)  309 us
  transfers between devices with their start and end apart: 6, of which 4 were waited for; matrix products, arithmetic and copies ran while one was open for 5% of the time, Pallas kernels for 0%

profile of v1, /device:TPU:32, one launch (start us, length us, event | category | flops | bytes accessed | tf_op | source)
XLA Modules:
  0.0 1622.0 jit_solution(9581043041494488295)
XLA Ops:
  8.1 1.5 fusion.84
  11.6 1.3 reduce_sum.112
  14.3 2.0 fusion.65
  17.0 1168.2 %all-reduce.6.cloned.1.call-done = f32[34,3072]{1,0:T(8,128)} async-done(((f32[34,3072]{1,0:T(8,128)}), f32[34,3072]{1,0:T(8,128)}) %all-reduce.6.cloned.1.call-update) | async-done | bytes 417808 | tf_op jit(solution)/shard_map/psum | solution.py:158
  1186.1 1.3 collective-permute-start
  1192.3 1.3 multiply_add_fusion.1
  1193.7 1.9 collective-permute-start.1
  1196.2 6.3 collective-permute-start.2
  1202.5 1.8 collective-permute-done.2
  1208.3 1.2 fusion.28
  1209.5 4.5 multiply_reduce_fusion
  1214.1 14.8 all-reduce.8.cloned.1.call-done
  1229.8 1.6 fusion.30
  1232.2 3.4 bitcast_reduce_fusion
  1236.4 1.1 fusion.23
  1237.5 4.4 add_convert_fusion
  1242.4 58.2 %while.11 = (s32[]{:T(128)}, bf16[8,256,128]{1,2,0:T(8,128)(2,1)}, s32[8]{0:T(128)}, bf16[256,1024]{1,0:T(8,128)(2,1)S(1)}, bf16[1024,1024]{0,1:T(8,128)(2,1)S(1...) while((s32[]{:T(128)}, bf16[8,256,128]{1,2,0:T(8,128)(2,1)}, ...), condition=%wide.region_15.16_spmd.clone, body=%wide.region_12.15_spmd.clone.sunk | while | flops 170786816 | bytes 4014055 | solution.py:84
  1242.4 1.2 dynamic_slice.86
  1245.2 1.3 fusion.102
  1247.6 1.3 fusion.104
  1249.7 1.2 dynamic_slice.86
  1252.5 1.3 fusion.102
  1253.8 1.1 fusion.103
  1254.9 1.3 fusion.104
  1257.0 1.2 dynamic_slice.86
  1259.7 1.3 fusion.102
  1262.1 1.3 fusion.104
  1264.2 1.2 dynamic_slice.86
  1267.0 1.3 fusion.102
  1269.4 1.3 fusion.104
  1271.5 1.2 dynamic_slice.86
  1274.3 1.3 fusion.102
  1275.6 1.1 fusion.103
  1276.7 1.3 fusion.104
  1278.8 1.2 dynamic_slice.86
  1281.6 1.3 fusion.102
  1282.9 1.1 fusion.103
  1284.0 1.3 fusion.104
  1286.1 1.2 dynamic_slice.86
  1288.8 1.3 fusion.102
  1291.3 1.3 fusion.104
  1293.3 1.2 dynamic_slice.86
  1296.1 1.3 fusion.102
  1297.4 1.1 fusion.103
  1298.5 1.3 fusion.104
  1300.6 308.8 %all-gather.2.cloned.1.call-done = bf16[2048,1024]{1,0:T(8,128)(2,1)} async-done(((bf16[8,1024]{1,0:T(8,128)(2,1)}), bf16[2048,1024]{1,0:T(8,128)(2,1)}) %all-gather.2.cloned.1.call-update) | async-done | bytes 4194320 | tf_op jit(solution)/shard_map/all_gather | solution.py:159
  1609.5 3.6 convolution_multiply_fusion.2
  1613.1 1.4 fusion.27
  (156 shorter events, 32.6 us)
Async XLA Ops:
  8.0 1177.7 %copy-start = (bf16[2048,32]{0,1:T(8,128)(2,1)S(1)}, bf16[2048,32]{0,1:T(8,128)(2,1)}, u32[]{:S(2)}) copy-start(bf16[2048,32]{0,1:T(8,128)(2,1)} %param.23) | copy-start | bytes 393220
  8.0 8.3 copy-start.1
  8.0 9.0 copy-start.8
  8.0 1177.2 %all-reduce.6.cloned.1.call-start = ((), (), s32[]{:S(2)}) async-start(), calls=%async_computation | async-start | bytes 983040 | tf_op jit(solution)/shard_map/psum | solution.py:158
  16.3 1172.4 %copy-start.12 = (f32[128]{0:T(128)S(1)}, f32[128]{0:T(128)}, u32[]{:S(2)}) copy-start(f32[128]{0:T(128)} %param.34) | copy-start | bytes 1540
  16.3 1172.4 %copy-start.13 = (f32[128]{0:T(128)S(1)}, f32[128]{0:T(128)}, u32[]{:S(2)}) copy-start(f32[128]{0:T(128)} %param.35) | copy-start | bytes 1540
  16.3 1172.5 %copy-start.2 = (bf16[256,1024]{1,0:T(8,128)(2,1)S(1)}, bf16[256,1024]{1,0:T(8,128)(2,1)}, u32[]{:S(2)}) copy-start(bf16[256,1024]{1,0:T(8,128)(2,1)} %param.36) | copy-start | bytes 1572868
  16.3 1212.6 %all-reduce.8.cloned.1.call-start = ((), (), s32[]{:S(2)}) async-start(), calls=%async_computation.1 | async-start | bytes 983040 | tf_op jit(solution)/shard_map/psum | solution.py:158
  1185.3 424.2 %all-gather.2.cloned.1.call-start = ((), (), s32[]{:S(2)}) async-start(), calls=%async_computation.2 | async-start | bytes 4210688 | tf_op jit(solution)/shard_map/all_gather | solution.py:159
  1186.1 6.2 collective-permute-start
  1188.8 0.8 copy-start.9
  1189.4 2.9 copy-start.10
  1193.7 8.8 collective-permute-start.1
  1196.2 8.2 collective-permute-start.2
  1205.4 1.1 copy-start.7
  1205.4 1.1 copy-start.11
  1206.0 2.3 copy-start.3
  1207.4 24.8 %copy-start.5 = (bf16[8,4,8,128]{3,2,1,0:T(8,128)(2,1)}, bf16[8,4,8,128]{3,2,1,0:T(8,128)(2,1)S(1)}, u32[]{:S(2)}) copy-start(bf16[8,4,8,128]{3,2,1,0:T(8,128)(2,1)S(1)} %convert_bitcast_fusion) | copy-start | bytes 196612
  1236.4 1.1 copy-start.6
  1609.5 3.6 copy-start.4
Sparse Core Ops, SparseCore 0:
  16.4 1168.7 all-reduce.5
  1188.0 40.8 all-reduce.7
Sparse Core Ops, SparseCore 1:
  1187.8 421.6 all-gather.1
